TPU v7x, 256 devices: a whole 4x4x8 slice. The times are simulated.
256 devices in a mesh: dp: 4 (over y), gx: 4 (over x), gy: 16 (over z, core).
Axes of the slice: x: 4, y: 4, z: 8, core: 2. Of those that a mesh axis runs over, the one named last changes fastest.
Arguments:
- field: bfloat16 [4, 64, 32, 20, 2048], P('dp', 'gx', 'gy'), may hold values from -6 to 6
- cotangent: bfloat16 [4, 64, 32, 20, 2048], P('dp', 'gx', 'gy'), may hold values from -6 to 6
- spectral_weight: bfloat16 [24, 24, 20, 20, 192], P(None, None, None, None, ('gx', 'gy')), may hold values from -2.5 to 2.5
- bypass_weight: bfloat16 [20, 20], replicated, may hold values from -1.25 to 1.25
Outputs:
- grad_field: bfloat16 [4, 64, 32, 20, 2048], P('dp', 'gx', 'gy')
- grad_spectral: float32 [24, 24, 20, 20, 192], P(None, None, None, None, ('gx', 'gy'))
- grad_bypass: float32 [20, 20], replicated
All inputs are finite; a program needn't handle non-finite values.
Results may differ from a plain program's by a relative error of at most 0.034.
Values may be sent and summed in bfloat16 or wider, within the bound.
No kernel may reach another device: no remote copies, remote signals or barrier semaphores. Data moves between devices by JAX's collectives and lax.ppermute only.
A program may use at most 192 MiB of HBM per device.

v0:
```python
import math
import jax
import jax.numpy as jnp
from jax import lax
from jax.sharding import PartitionSpec as P

MX = 12
MY = 12
MZ = 12
MT = 4
NZ = 128
NT = 16


def basis(length, kept):
    places = lax.iota(jnp.int32, length)
    orders = lax.iota(jnp.int32, kept)
    cos_arg = places[:, None] * orders[None, :] % length
    sin_arg = places[:, None] * (orders[None, :] + 1) % length
    step_angle = 2.0 * math.pi / length
    scale = math.sqrt(2.0 / length)
    cos_part = jnp.cos(cos_arg.astype(jnp.float32) * step_angle)
    sin_part = jnp.sin(sin_arg.astype(jnp.float32) * step_angle)
    return jnp.concatenate([cos_part, sin_part], axis=1) * scale


def mode_dot(form, data, table):
    upper = table.astype(jnp.bfloat16)
    lower = (table - upper.astype(jnp.float32)).astype(jnp.bfloat16)
    first = jnp.einsum(form, data, upper, preferred_element_type=jnp.float32)
    return first + jnp.einsum(form, data, lower, preferred_element_type=jnp.float32)


def body(field, cotangent, spectral_weight, bypass_weight):
    cells_x = field.shape[1]
    cells_y = field.shape[2]
    channels = field.shape[3]
    parts_x = lax.axis_size("gx")
    parts_y = lax.axis_size("gy")
    table_x = basis(cells_x * parts_x, MX)
    table_y = basis(cells_y * parts_y, MY)
    table_z = basis(NZ, MZ)
    table_t = basis(NT, MT)
    modes_zt = 4 * MZ * MT
    table_zt = (table_z[:, None, :, None] * table_t[None, :, None, :]).reshape(NZ * NT, modes_zt)

    def analyze(cells):
        matrix = cells.reshape(-1, NZ * NT)
        coeff = mode_dot("rp,pq->rq", matrix, table_zt).astype(jnp.bfloat16)
        coeff = coeff.reshape(cells_x, cells_y, channels, modes_zt)
        along_x = lax.all_to_all(coeff, "gx", split_axis=3, concat_axis=0, tiled=True)
        partial_x = mode_dot("xycq,xk->kycq", along_x, table_x).astype(jnp.bfloat16)
        along_y = lax.all_to_all(partial_x, "gy", split_axis=3, concat_axis=1, tiled=True)
        return mode_dot("kycq,yl->klcq", along_y, table_y).astype(jnp.bfloat16)

    def synthesize(spectrum):
        partial_y = mode_dot("klcq,yl->kycq", spectrum, table_y).astype(jnp.bfloat16)
        returned = lax.all_to_all(partial_y, "gy", split_axis=1, concat_axis=3, tiled=True)
        partial_x = mode_dot("kycq,xk->xycq", returned, table_x).astype(jnp.bfloat16)
        coeff = lax.all_to_all(partial_x, "gx", split_axis=0, concat_axis=3, tiled=True)
        matrix = coeff.reshape(-1, modes_zt)
        values = mode_dot("rq,pq->rp", matrix, table_zt)
        return values.reshape(1, cells_x, cells_y, channels, NZ * NT)

    spectrum = analyze(field)
    mixed = jnp.einsum(
        "klcq,klcoq->kloq", spectrum, spectral_weight, preferred_element_type=jnp.float32
    ).astype(jnp.bfloat16)
    spatial = synthesize(mixed)
    bypass = jnp.einsum("bxyip,io->bxyop", field, bypass_weight, preferred_element_type=jnp.float32)
    pre = spatial + bypass
    unused, pullback = jax.vjp(jax.nn.gelu, pre)
    (slope,) = pullback(cotangent.astype(jnp.float32))
    upstream = slope.astype(jnp.bfloat16)
    bypass_term = jnp.einsum("bxyip,bxyop->io", field, upstream, preferred_element_type=jnp.float32)
    grad_bypass = lax.psum(bypass_term, ("dp", "gx", "gy"))
    spectrum_up = analyze(upstream)
    local_grad = jnp.einsum(
        "klcq,kloq->klcoq", spectrum, spectrum_up, preferred_element_type=jnp.float32
    )
    grad_spectral = lax.psum(local_grad.astype(jnp.bfloat16), "dp").astype(jnp.float32)
    spectrum_back = jnp.einsum(
        "kloq,klcoq->klcq", spectrum_up, spectral_weight, preferred_element_type=jnp.float32
    ).astype(jnp.bfloat16)
    through_bypass = jnp.einsum(
        "bxyop,io->bxyip", upstream, bypass_weight, preferred_element_type=jnp.float32
    )
    grad_field = (synthesize(spectrum_back) + through_bypass).astype(jnp.bfloat16)
    return (grad_field, grad_spectral, grad_bypass)


def solution(mesh):
    in_specs = (
        P("dp", "gx", "gy", None, None),
        P("dp", "gx", "gy", None, None),
        P(None, None, None, None, ("gx", "gy")),
        P(),
    )
    out_specs = (P("dp", "gx", "gy", None, None), P(None, None, None, None, ("gx", "gy")), P())
    return jax.shard_map(body, mesh=mesh, in_specs=in_specs, out_specs=out_specs, check_vma=False)
```

profile of v0, /device:TPU:1, one launch (start us, length us, event | category | flops | bytes accessed | tf_op | source)
XLA Modules:
  0.0 493.5 jit_solution(16601009664940160456)
XLA Ops:
  7.5 4.7 copy.145
  15.8 6.2 %fusion = (bf16[128,16,24,8]{1,0,3,2:T(8,128)(2,1)}, bf16[128,16,24,8]{1,0,3,2:T(8,128)(2,1)}) fusion(f32[16,8]{0,1:T(8,128)S(1)} %maximum_multiply_fusion.3, f32[128,24]{0,1:T(8,128)S(1)} %maximum_multiply_fusion.2), kind=kLoop, calls=%fused_computation.5 | loop fusion | flops 1966080 | bytes 1585664 | tf_op jit(solution)/shard_map/convert_element_type | solution.py:29
  22.0 11.6 %convert_element_type.256 = bf16[2048,192]{0,1:T(8,128)(2,1)S(1)} reshape(bf16[128,16,24,8]{1,0,3,2:T(8,128)(2,1)} %get-tuple-element.26) | data formatting | bytes 1572864 | tf_op jit(solution)/shard_map/convert_element_type | solution.py:29
  33.7 12.3 %convert_element_type.253 = bf16[2048,192]{0,1:T(8,128)(2,1)} reshape(bf16[128,16,24,8]{1,0,3,2:T(8,128)(2,1)} %get-tuple-element.27) | data formatting | bytes 1572864 | tf_op jit(solution)/shard_map/convert_element_type | solution.py:28
  49.9 5.9 %reshape.160 = bf16[16,2,20,192]{2,1,0,3:T(2,128)(2,1)S(1)} reshape(bf16[640,192]{0,1:T(8,128)(2,1)} %fusion.30) | data formatting | bytes 491520 | tf_op jit(solution)/shard_map/reshape | solution.py:50
  55.9 4.2 reshape.162
  60.0 4.8 all-to-all-start
  65.0 5.3 %all-to-all-done = bf16[4,2,15360]{2,1,0:T(2,128)(2,1)S(1)} async-done(((bf16[4,2,15360]{2,1,0:T(2,128)(2,1)}), bf16[4,2,15360]{2,1,0:T(2,128)(2,1)S(1)}, u32[]{:S(2)}, u32[]{:S(2)}) %all-to-all-start) | async-done | bytes 245792 | tf_op jit(solution)/shard_map/all_to_all | solution.py:51
  70.3 4.1 reshape.163
  79.3 10.9 %all-to-all-start.1 = ((bf16[16,2,1440]{2,1,0:T(2,128)(2,1)}), bf16[16,2,1440]{2,1,0:T(2,128)(2,1)S(1)}, u32[]{:S(2)}, u32[]{:S(2)}) async-start(bf16[16,2,1440]{2,1,0:T(2,128)(2,1)} %reshape.164), calls=%async_computation.1 | async-start | bytes 196608 | tf_op jit(solution)/shard_map/all_to_all | solution.py:53
  90.4 8.2 %all-to-all-done.1 = bf16[16,2,1440]{2,1,0:T(2,128)(2,1)S(1)} async-done(((bf16[16,2,1440]{2,1,0:T(2,128)(2,1)}), bf16[16,2,1440]{2,1,0:T(2,128)(2,1)S(1)}, u32[]{:S(2)}, u32[]{:S(2)}) %all-to-all-start.1) | async-done | bytes 92192 | tf_op jit(solution)/shard_map/all_to_all | solution.py:53
  101.2 5.0 %multiply_reduce_fusion.1 = bf16[24,24,3,20]{1,0,2,3:T(8,128)(2,1)S(1)} fusion(f32[24,24,3,20]{1,0,2,3:T(8,128)S(1)} %copy.223, bf16[24,24,20,20,3]{1,0,4,3,2:T(8,128)(2,1)} %param.6), kind=kLoop, calls=%fused_computation.3 | loop fusion | flops 2039040 | bytes 1589760 | tf_op jit(solution)/shard_map/klcq,klcoq->kloq/dot_general | solution.py:66
  107.7 10.9 %all_to_all.138 = bf16[16,2,1440]{2,1,0:T(2,128)(2,1)S(1)} all-to-all(bf16[16,2,1440]{2,1,0:T(2,128)(2,1)S(1)} %reshape.166), channel_id=1, replica_groups=mesh['dp'=4,'gx'=4,'gy'=16] {'gy'}, dimensions={0} | all-to-all | bytes 184320 | tf_op jit(solution)/shard_map/all_to_all | solution.py:58
  122.3 9.6 %all_to_all.139 = bf16[4,2,15360]{2,1,0:T(2,128)(2,1)S(1)} all-to-all(bf16[4,2,15360]{2,1,0:T(2,128)(2,1)S(1)} %reshape.168), channel_id=1, replica_groups=mesh['dp'=4,'gx'=4,'gy'=16] {'gx'}, dimensions={0} | all-to-all | bytes 491520 | tf_op jit(solution)/shard_map/all_to_all | solution.py:60
  139.5 6.7 %reshape.142 = f32[1,16,2,20,2048]{4,3,2,1,0:T(8,128)} reshape(f32[640,2048]{1,0:T(8,128)} %convolution_add_fusion.1) | data formatting | bytes 10485760 | tf_op jit(solution)/shard_map/reshape | solution.py:63
  146.1 11.0 %fusion.4 = bf16[1,16,2,20,2048]{4,3,2,1,0:T(8,128)(2,1)} fusion(f32[1,16,2,20,2048]{4,3,2,1,0:T(8,128)} %reshape.142, bf16[1,16,2,20,2048]{4,2,3,1,0:T(2,128)(2,1)} %param.5, bf16[16,2,20,2048]{3,1,2,0:T(2,128)(2,1)} %bitcast.208, bf16[20,20]{1,0:T(8,128)(2,1)S(1)} %copy-done), kind=kOutput, calls=%fused_computation.13 | convolution fusion | flops 81264640 | bytes 13108000 | tf_op jit(solution)/shard_map/bxyip,io->bxyop/dot_general | solution.py:70
  157.1 5.3 %reshape.144 = bf16[640,2048]{1,0:T(8,128)(2,1)} reshape(bf16[1,16,2,20,2048]{4,3,2,1,0:T(8,128)(2,1)} %fusion.4) | data formatting | bytes 5242880 | tf_op jit(solution)/shard_map/reshape | solution.py:48
  168.0 3.8 reshape.161
  175.3 8.8 %all_to_all.140 = bf16[4,2,15360]{2,1,0:T(2,128)(2,1)} all-to-all(bf16[4,2,15360]{2,1,0:T(2,128)(2,1)S(1)} %reshape.170), channel_id=1, replica_groups=mesh['dp'=4,'gx'=4,'gy'=16] {'gx'}, dimensions={0} | all-to-all | bytes 491520 | tf_op jit(solution)/shard_map/all_to_all | solution.py:51
  184.2 6.0 %reshape.171 = bf16[192,16,2,20]{3,2,1,0:T(2,128)(2,1)S(1)} reshape(bf16[4,2,15360]{2,1,0:T(2,128)(2,1)} %all_to_all.140) | data formatting | bytes 491520
  196.9 5.2 %all-to-all-start.5 = ((bf16[16,2,1440]{2,1,0:T(2,128)(2,1)}), bf16[16,2,1440]{2,1,0:T(2,128)(2,1)S(1)}, u32[]{:S(2)}, u32[]{:S(2)}) async-start(bf16[16,2,1440]{2,1,0:T(2,128)(2,1)} %reshape.172), calls=%async_computation.5 | async-start | bytes 196608 | tf_op jit(solution)/shard_map/all_to_all | solution.py:53
  204.3 6.3 %all-to-all-done.5 = bf16[16,2,1440]{2,1,0:T(2,128)(2,1)S(1)} async-done(((bf16[16,2,1440]{2,1,0:T(2,128)(2,1)}), bf16[16,2,1440]{2,1,0:T(2,128)(2,1)S(1)}, u32[]{:S(2)}, u32[]{:S(2)}) %all-to-all-start.5) | async-done | bytes 92192 | tf_op jit(solution)/shard_map/all_to_all | solution.py:53
  214.5 5.0 %multiply_reduce_fusion = bf16[24,24,3,20]{1,0,2,3:T(8,128)(2,1)S(1)} fusion(f32[24,24,3,20]{1,0,2,3:T(8,128)S(1)} %copy.224, bf16[24,24,20,20,3]{1,0,4,3,2:T(8,128)(2,1)} %param.6), kind=kLoop, calls=%fused_computation.2 | loop fusion | flops 2039040 | bytes 1589760 | tf_op jit(solution)/shard_map/kloq,klcoq->klcq/dot_general | solution.py:82
  221.6 3.7 all-to-all-start.6
  225.3 4.9 fusion.31
  230.2 76.2 %psum.15 = f32[20,20]{0,1:T(8,128)S(1)} all-reduce(f32[20,20]{0,1:T(8,128)S(1)} %fusion.31), channel_id=1, replica_groups=mesh['dp'=4,'gx'=4,'gy'=16] {'dp','gx','gy'}, use_global_device_ids=true, to_apply=%region_1.2 | all-reduce | flops 400 | bytes 3200 | tf_op jit(solution)/shard_map/psum | solution.py:76
  321.4 5.3 %fusion.1 = bf16[24,24,20,20,3]{1,0,4,3,2:T(8,128)(2,1)} fusion(f32[24,24,3,20]{1,0,2,3:T(8,128)S(1)} %copy-done.3, f32[24,24,3,20]{1,0,2,3:T(8,128)} %copy.186), kind=kLoop, calls=%fused_computation.10 | loop fusion | flops 1382400 | bytes 1658880 | tf_op jit(solution)/shard_map/convert_element_type | solution.py:81
  334.4 7.2 %reshape.147 = f32[1,16,2,20,2048]{4,3,2,1,0:T(8,128)} reshape(f32[640,2048]{1,0:T(8,128)} %convolution_add_fusion) | data formatting | bytes 10485760 | tf_op jit(solution)/shard_map/reshape | solution.py:63
  341.6 4.1 fusion.12
  345.7 4.2 copy.189
  349.9 126.0 %all-reduce.2.cloned.1.call-done = bf16[24,24,20,20,3]{1,0,4,3,2:T(8,128)(2,1)} async-done(((bf16[24,24,20,20,3]{1,0,4,3,2:T(8,128)(2,1)}), bf16[24,24,20,20,3]{1,0,4,3,2:T(8,128)(2,1)}) %all-reduce.2.cloned.1.call-update) | async-done | bytes 1382416 | tf_op jit(solution)/shard_map/psum | solution.py:81
  475.9 10.2 %convert_element_type.284 = f32[24,24,20,20,3]{1,0,4,3,2:T(8,128)} convert(bf16[24,24,20,20,3]{1,0,4,3,2:T(8,128)(2,1)} %all-reduce.2.cloned.1.call-done) | non-fusion elementwise | flops 691200 | bytes 4147200 | tf_op jit(solution)/shard_map/convert_element_type | solution.py:81
  (90 shorter events, 74.8 us)
Async XLA Ops:
  7.2 139.0 %copy-start = (bf16[20,20]{1,0:T(8,128)(2,1)S(1)}, bf16[20,20]{1,0:T(8,128)(2,1)}, u32[]{:S(2)}) copy-start(bf16[20,20]{1,0:T(8,128)(2,1)} %param.7) | copy-start | bytes 2404
  60.0 10.3 %all-to-all-start = ((bf16[4,2,15360]{2,1,0:T(2,128)(2,1)}), bf16[4,2,15360]{2,1,0:T(2,128)(2,1)S(1)}, u32[]{:S(2)}, u32[]{:S(2)}) async-start(bf16[4,2,15360]{2,1,0:T(2,128)(2,1)} %reshape.162), calls=%async_computation | async-start | bytes 491520 | tf_op jit(solution)/shard_map/all_to_all | solution.py:51
  79.3 19.3 %all-to-all-start.1 = ((bf16[16,2,1440]{2,1,0:T(2,128)(2,1)}), bf16[16,2,1440]{2,1,0:T(2,128)(2,1)S(1)}, u32[]{:S(2)}, u32[]{:S(2)}) async-start(bf16[16,2,1440]{2,1,0:T(2,128)(2,1)} %reshape.164), calls=%async_computation.1 | async-start | bytes 196608 | tf_op jit(solution)/shard_map/all_to_all | solution.py:53
  119.1 16.2 %copy-start.1 = (bf16[2048,192]{0,1:T(8,128)(2,1)S(1)}, bf16[2048,192]{0,1:T(8,128)(2,1)}, u32[]{:S(2)}) copy-start(bf16[2048,192]{0,1:T(8,128)(2,1)} %convert_element_type.253) | copy-start | bytes 2359300
  196.9 13.7 %all-to-all-start.5 = ((bf16[16,2,1440]{2,1,0:T(2,128)(2,1)}), bf16[16,2,1440]{2,1,0:T(2,128)(2,1)S(1)}, u32[]{:S(2)}, u32[]{:S(2)}) async-start(bf16[16,2,1440]{2,1,0:T(2,128)(2,1)} %reshape.172), calls=%async_computation.5 | async-start | bytes 196608 | tf_op jit(solution)/shard_map/all_to_all | solution.py:53
  221.6 87.7 %all-to-all-start.6 = ((bf16[16,2,1440]{2,1,0:T(2,128)(2,1)}), bf16[16,2,1440]{2,1,0:T(2,128)(2,1)S(1)}, u32[]{:S(2)}, u32[]{:S(2)}) async-start(bf16[16,2,1440]{2,1,0:T(2,128)(2,1)} %reshape.174), calls=%async_computation.6 | async-start | bytes 196608 | tf_op jit(solution)/shard_map/all_to_all | solution.py:58
  230.2 91.2 %copy-start.3 = (f32[24,24,3,20]{1,0,2,3:T(8,128)S(1)}, f32[24,24,3,20]{1,0,2,3:T(8,128)}, u32[]{:S(2)}) copy-start(f32[24,24,3,20]{1,0,2,3:T(8,128)} %copy.187) | copy-start | bytes 414724
  317.9 9.0 %all-to-all-start.7 = ((bf16[4,2,15360]{2,1,0:T(2,128)(2,1)}), bf16[4,2,15360]{2,1,0:T(2,128)(2,1)S(1)}, u32[]{:S(2)}, u32[]{:S(2)}) async-start(bf16[4,2,15360]{2,1,0:T(2,128)(2,1)} %reshape.176), calls=%async_computation.7 | async-start | bytes 491520 | tf_op jit(solution)/shard_map/all_to_all | solution.py:60
  321.3 154.6 %all-reduce.2.cloned.1.call-start = ((), (), s32[]{:S(2)}) async-start(), calls=%async_computation.8 | async-start | bytes 14745600 | tf_op jit(solution)/shard_map/psum | solution.py:81
  334.4 7.2 %copy-start.2 = (bf16[1,16,2,20,2048]{4,3,2,1,0:T(8,128)(2,1)S(1)}, bf16[1,16,2,20,2048]{4,3,2,1,0:T(8,128)(2,1)}, u32[]{:S(2)}) copy-start(bf16[1,16,2,20,2048]{4,3,2,1,0:T(8,128)(2,1)} %fusion.4) | copy-start | bytes 7864324
Sparse Core Ops, SparseCore 0:
  326.8 149.0 all-reduce.1
where the time goes:
time: 503 us; the launch traced here: 493 us
  waiting for transfers between devices  146 us (29%)
  local copies, waits for them, and re-layouts  120 us (24%)
  blocking collectives  105 us (21%)
  matrix products  46.5 us (9%)
  other arithmetic  32.3 us (6%)
  starting transfers between devices  28 us (6%)
  between operations  15.1 us (3%)
    psum x1, waiting for transfers between devices, body(): lax.psum(local_grad.astype(jnp.bfloat16), 'dp').astype(jnp.float32)  126 us
    psum x1, blocking collectives, body(): grad_bypass = lax.psum(bypass_term, ('dp', 'gx', 'gy'))  76.2 us
    unnamed x29, local copies, waits for them, and re-layouts  39.6 us
    dot_general x12, matrix products, mode_dot(): jnp.einsum(form, data, lower, preferred_element_type=jnp.float32)  16.9 us
    all_to_all x2, starting transfers between devices, analyze(): lax.all_to_all(partial_x, 'gy', split_axis=3, concat_axis=1, tiled=True)  16.1 us
    all_to_all x2, waiting for transfers between devices, analyze(): lax.all_to_all(partial_x, 'gy', split_axis=3, concat_axis=1, tiled=True)  14.5 us
    reshape x2, local copies, waits for them, and re-layouts, synthesize(): return values.reshape(1, cells_x, cells_y, channels, NZ * NT)  13.9 us
    convert_element_type x1, local copies, waits for them, and re-layouts, mode_dot(): upper = table.astype(jnp.bfloat16)  12.3 us
  transfers between devices with their start and end apart: 6, of which 5 were waited for; matrix products, arithmetic and copies ran while one was open for 8% of the time, Pallas kernels for 0%

commit v1 on v0

--- a/solution.py
+++ b/solution.py
@@ -78,7 +78,9 @@
     local_grad = jnp.einsum(
         "klcq,kloq->klcoq", spectrum, spectrum_up, preferred_element_type=jnp.float32
     )
-    grad_spectral = lax.psum(local_grad.astype(jnp.bfloat16), "dp").astype(jnp.float32)
+    grad_spectral = jnp.sum(lax.all_gather(local_grad.astype(jnp.bfloat16), "dp"), axis=0).astype(
+        jnp.float32
+    )
     spectrum_back = jnp.einsum(
         "kloq,klcoq->klcq", spectrum_up, spectral_weight, preferred_element_type=jnp.float32
     ).astype(jnp.bfloat16)

time: 503 us -> 520 us (1.034)
  other arithmetic: 32.3 us -> 47.7 us
  blocking collectives: 105 us -> 118 us
    psum x1 -> x0, waiting for transfers between devices: 126 us -> none  [body(): lax.psum(local_grad.astype(jnp.bfloat16), 'dp').astype(jnp.float32)]
    all_gather x0 -> x1, waiting for transfers between devices: none -> 126 us  [body(): lax.all_gather(local_grad.astype(jnp.bfloat16), 'dp')]
    reduce_sum x0 -> x1, other arithmetic: none -> 15.3 us  [body(): jnp.sum(lax.all_gather(local_grad.astype(jnp.bfloat16), 'dp'), axis=0)]
    all_to_all x1 -> x2, blocking collectives: 10.9 us -> 21.6 us  [synthesize(): lax.all_to_all(partial_y, 'gy', split_axis=1, concat_axis=3, tiled=True)]
  transfers between devices with their start and end apart: 6 -> 5, of which waited for: 5 -> 4; matrix products, arithmetic and copies ran while one was open for 8% -> 8% of each run, Pallas kernels for 0% -> 0%
where the time goes in v1:
time: 520 us; the launch traced here: 511 us
  waiting for transfers between devices  146 us (28%)
  blocking collectives  118 us (23%)
  local copies, waits for them, and re-layouts  116 us (22%)
  other arithmetic  47.7 us (9%)
  matrix products  44.2 us (8%)
  starting transfers between devices  24.4 us (5%)
  between operations  14.7 us (3%)
    all_gather x1, waiting for transfers between devices, body(): lax.all_gather(local_grad.astype(jnp.bfloat16), 'dp')  126 us
    psum x1, blocking collectives, body(): grad_bypass = lax.psum(bypass_term, ('dp', 'gx', 'gy'))  78.4 us
    unnamed x29, local copies, waits for them, and re-layouts  37.9 us
    all_to_all x2, blocking collectives, synthesize(): lax.all_to_all(partial_y, 'gy', split_axis=1, concat_axis=3, tiled=True)  21.6 us
    all_to_all x2, starting transfers between devices, analyze(): lax.all_to_all(partial_x, 'gy', split_axis=3, concat_axis=1, tiled=True)  16.1 us
    reduce_sum x1, other arithmetic, body(): jnp.sum(lax.all_gather(local_grad.astype(jnp.bfloat16), 'dp'), axis=0)  15.3 us
    dot_general x12, matrix products, mode_dot(): jnp.einsum(form, data, lower, preferred_element_type=jnp.float32)  15.2 us
    all_to_all x2, waiting for transfers between devices, analyze(): lax.all_to_all(partial_x, 'gy', split_axis=3, concat_axis=1, tiled=True)  14.5 us
  transfers between devices with their start and end apart: 5, of which 4 were waited for; matrix products, arithmetic and copies ran while one was open for 8% of the time, Pallas kernels for 0%

profile of v1, /device:TPU:1, one launch (start us, length us, event | category | flops | bytes accessed | tf_op | source)
XLA Modules:
  0.0 510.9 jit_solution(8396642702293125426)
XLA Ops:
  7.5 4.7 copy.145
  15.8 6.2 %fusion = (bf16[128,16,24,8]{1,0,3,2:T(8,128)(2,1)}, bf16[128,16,24,8]{1,0,3,2:T(8,128)(2,1)}) fusion(f32[16,8]{0,1:T(8,128)S(1)} %maximum_multiply_fusion.3, f32[128,24]{0,1:T(8,128)S(1)} %maximum_multiply_fusion.2), kind=kLoop, calls=%fused_computation.5 | loop fusion | flops 1966080 | bytes 1585664 | tf_op jit(solution)/shard_map/convert_element_type | solution.py:29
  22.0 11.6 %convert_element_type.258 = bf16[2048,192]{0,1:T(8,128)(2,1)S(1)} reshape(bf16[128,16,24,8]{1,0,3,2:T(8,128)(2,1)} %get-tuple-element.26) | data formatting | bytes 1572864 | tf_op jit(solution)/shard_map/convert_element_type | solution.py:29
  33.7 12.3 %convert_element_type.255 = bf16[2048,192]{0,1:T(8,128)(2,1)} reshape(bf16[128,16,24,8]{1,0,3,2:T(8,128)(2,1)} %get-tuple-element.27) | data formatting | bytes 1572864 | tf_op jit(solution)/shard_map/convert_element_type | solution.py:28
  49.9 6.0 %reshape.161 = bf16[16,2,20,192]{2,1,0,3:T(2,128)(2,1)S(1)} reshape(bf16[640,192]{0,1:T(8,128)(2,1)} %fusion.30) | data formatting | bytes 491520 | tf_op jit(solution)/shard_map/reshape | solution.py:50
  55.9 4.2 reshape.163
  60.1 4.8 all-to-all-start
  65.1 5.3 %all-to-all-done = bf16[4,2,15360]{2,1,0:T(2,128)(2,1)S(1)} async-done(((bf16[4,2,15360]{2,1,0:T(2,128)(2,1)}), bf16[4,2,15360]{2,1,0:T(2,128)(2,1)S(1)}, u32[]{:S(2)}, u32[]{:S(2)}) %all-to-all-start) | async-done | bytes 245792 | tf_op jit(solution)/shard_map/all_to_all | solution.py:51
  70.4 4.1 reshape.164
  79.3 11.0 %all-to-all-start.1 = ((bf16[16,2,1440]{2,1,0:T(2,128)(2,1)}), bf16[16,2,1440]{2,1,0:T(2,128)(2,1)S(1)}, u32[]{:S(2)}, u32[]{:S(2)}) async-start(bf16[16,2,1440]{2,1,0:T(2,128)(2,1)} %reshape.165), calls=%async_computation.1 | async-start | bytes 196608 | tf_op jit(solution)/shard_map/all_to_all | solution.py:53
  90.5 8.2 %all-to-all-done.1 = bf16[16,2,1440]{2,1,0:T(2,128)(2,1)S(1)} async-done(((bf16[16,2,1440]{2,1,0:T(2,128)(2,1)}), bf16[16,2,1440]{2,1,0:T(2,128)(2,1)S(1)}, u32[]{:S(2)}, u32[]{:S(2)}) %all-to-all-start.1) | async-done | bytes 92192 | tf_op jit(solution)/shard_map/all_to_all | solution.py:53
  101.2 5.0 multiply_reduce_fusion.1
  107.7 10.9 %all_to_all.138 = bf16[16,2,1440]{2,1,0:T(2,128)(2,1)S(1)} all-to-all(bf16[16,2,1440]{2,1,0:T(2,128)(2,1)S(1)} %reshape.167), channel_id=1, replica_groups=mesh['dp'=4,'gx'=4,'gy'=16] {'gy'}, dimensions={0} | all-to-all | bytes 184320 | tf_op jit(solution)/shard_map/all_to_all | solution.py:58
  122.4 9.6 %all_to_all.139 = bf16[4,2,15360]{2,1,0:T(2,128)(2,1)S(1)} all-to-all(bf16[4,2,15360]{2,1,0:T(2,128)(2,1)S(1)} %reshape.169), channel_id=1, replica_groups=mesh['dp'=4,'gx'=4,'gy'=16] {'gx'}, dimensions={0} | all-to-all | bytes 491520 | tf_op jit(solution)/shard_map/all_to_all | solution.py:60
  139.6 6.7 %reshape.142 = f32[1,16,2,20,2048]{4,3,2,1,0:T(8,128)} reshape(f32[640,2048]{1,0:T(8,128)} %convolution_add_fusion.1) | data formatting | bytes 10485760 | tf_op jit(solution)/shard_map/reshape | solution.py:63
  146.3 11.0 %fusion.4 = bf16[1,16,2,20,2048]{4,3,2,1,0:T(8,128)(2,1)} fusion(f32[1,16,2,20,2048]{4,3,2,1,0:T(8,128)} %reshape.142, bf16[1,16,2,20,2048]{4,2,3,1,0:T(2,128)(2,1)} %param.5, bf16[16,2,20,2048]{3,1,2,0:T(2,128)(2,1)} %bitcast.210, bf16[20,20]{1,0:T(8,128)(2,1)S(1)} %copy-done), kind=kOutput, calls=%fused_computation.13 | convolution fusion | flops 81264640 | bytes 13108000 | tf_op jit(solution)/shard_map/bxyip,io->bxyop/dot_general | solution.py:70
  157.3 5.3 %reshape.144 = bf16[640,2048]{1,0:T(8,128)(2,1)} reshape(bf16[1,16,2,20,2048]{4,3,2,1,0:T(8,128)(2,1)} %fusion.4) | data formatting | bytes 5242880 | tf_op jit(solution)/shard_map/reshape | solution.py:48
  175.5 8.8 %all_to_all.140 = bf16[4,2,15360]{2,1,0:T(2,128)(2,1)} all-to-all(bf16[4,2,15360]{2,1,0:T(2,128)(2,1)S(1)} %reshape.171), channel_id=1, replica_groups=mesh['dp'=4,'gx'=4,'gy'=16] {'gx'}, dimensions={0} | all-to-all | bytes 491520 | tf_op jit(solution)/shard_map/all_to_all | solution.py:51
  184.3 6.0 %reshape.172 = bf16[192,16,2,20]{3,2,1,0:T(2,128)(2,1)S(1)} reshape(bf16[4,2,15360]{2,1,0:T(2,128)(2,1)} %all_to_all.140) | data formatting | bytes 491520
  197.1 5.2 %all-to-all-start.5 = ((bf16[16,2,1440]{2,1,0:T(2,128)(2,1)}), bf16[16,2,1440]{2,1,0:T(2,128)(2,1)S(1)}, u32[]{:S(2)}, u32[]{:S(2)}) async-start(bf16[16,2,1440]{2,1,0:T(2,128)(2,1)} %reshape.173), calls=%async_computation.5 | async-start | bytes 196608 | tf_op jit(solution)/shard_map/all_to_all | solution.py:53
  204.5 6.2 %all-to-all-done.5 = bf16[16,2,1440]{2,1,0:T(2,128)(2,1)S(1)} async-done(((bf16[16,2,1440]{2,1,0:T(2,128)(2,1)}), bf16[16,2,1440]{2,1,0:T(2,128)(2,1)S(1)}, u32[]{:S(2)}, u32[]{:S(2)}) %all-to-all-start.5) | async-done | bytes 92192 | tf_op jit(solution)/shard_map/all_to_all | solution.py:53
  214.7 5.4 %fusion.1 = bf16[24,24,20,20,3]{1,0,4,3,2:T(8,128)(2,1)} fusion(f32[24,24,3,20]{1,0,2,3:T(8,128)} %copy.187, f32[24,24,3,20]{1,0,2,3:T(8,128)S(1)} %copy.186), kind=kLoop, calls=%fused_computation.10 | loop fusion | flops 1382400 | bytes 1658880 | tf_op jit(solution)/shard_map/convert_element_type | solution.py:81
  220.4 5.0 multiply_reduce_fusion
  226.9 10.8 %all_to_all.141 = bf16[16,2,1440]{2,1,0:T(2,128)(2,1)S(1)} all-to-all(bf16[16,2,1440]{2,1,0:T(2,128)(2,1)S(1)} %reshape.175), channel_id=1, replica_groups=mesh['dp'=4,'gx'=4,'gy'=16] {'gy'}, dimensions={0} | all-to-all | bytes 184320 | tf_op jit(solution)/shard_map/all_to_all | solution.py:58
  245.5 5.1 %fusion.31 = f32[20,20]{0,1:T(8,128)S(1)} fusion(bf16[16,2,20,2048]{3,1,2,0:T(2,128)(2,1)} %bitcast.211, bf16[1,16,2,20,2048]{4,3,2,1,0:T(8,128)(2,1)} %fusion.4), kind=kOutput, calls=%fused_computation.54 | convolution fusion | flops 52428800 | bytes 5244480 | tf_op jit(solution)/shard_map/bxyip,bxyop->io/dot_general | solution.py:75
  250.6 78.4 %psum.7 = f32[20,20]{0,1:T(8,128)S(1)} all-reduce(f32[20,20]{0,1:T(8,128)S(1)} %fusion.31), channel_id=1, replica_groups=mesh['dp'=4,'gx'=4,'gy'=16] {'dp','gx','gy'}, use_global_device_ids=true, to_apply=%region_1.2 | all-reduce | flops 400 | bytes 3200 | tf_op jit(solution)/shard_map/psum | solution.py:76
  337.2 7.0 %reshape.147 = f32[1,16,2,20,2048]{4,3,2,1,0:T(8,128)} reshape(f32[640,2048]{1,0:T(8,128)} %convolution_add_fusion) | data formatting | bytes 10485760 | tf_op jit(solution)/shard_map/reshape | solution.py:63
  344.2 4.1 fusion.12
  348.3 4.2 copy.189
  352.6 125.8 %all-gather.3.cloned.1.call-done = bf16[96,24,20,20,3]{1,0,4,3,2:T(8,128)(2,1)} async-done(((bf16[24,24,20,20,3]{1,0,4,3,2:T(8,128)(2,1)}), bf16[96,24,20,20,3]{1,0,4,3,2:T(8,128)(2,1)}) %all-gather.3.cloned.1.call-update) | async-done | bytes 5529616 | tf_op jit(solution)/shard_map/all_gather | solution.py:81
  478.3 15.3 %reduce_sum.12 = bf16[24,24,20,20,3]{1,0,4,3,2:T(8,128)(2,1)} reduce(bf16[4,24,24,20,20,3]{2,1,0,5,4,3:T(8,128)(2,1)} %bitcast.197, bf16[]{:T(256)} %constant.110.clone.1), dimensions={0}, to_apply=%region_0.1 | reduce | flops 2073600 | bytes 6912002 | tf_op jit(solution)/shard_map/reduce_sum | solution.py:81
  493.7 10.2 %convert_element_type.286 = f32[24,24,20,20,3]{1,0,4,3,2:T(8,128)} convert(bf16[24,24,20,20,3]{1,0,4,3,2:T(8,128)(2,1)} %reduce_sum.12) | non-fusion elementwise | flops 691200 | bytes 4147200 | tf_op jit(solution)/shard_map/convert_element_type | solution.py:81
  (90 shorter events, 71.6 us)
Async XLA Ops:
  7.2 139.1 %copy-start = (bf16[20,20]{1,0:T(8,128)(2,1)S(1)}, bf16[20,20]{1,0:T(8,128)(2,1)}, u32[]{:S(2)}) copy-start(bf16[20,20]{1,0:T(8,128)(2,1)} %param.7) | copy-start | bytes 2404
  60.1 10.3 %all-to-all-start = ((bf16[4,2,15360]{2,1,0:T(2,128)(2,1)}), bf16[4,2,15360]{2,1,0:T(2,128)(2,1)S(1)}, u32[]{:S(2)}, u32[]{:S(2)}) async-start(bf16[4,2,15360]{2,1,0:T(2,128)(2,1)} %reshape.163), calls=%async_computation | async-start | bytes 491520 | tf_op jit(solution)/shard_map/all_to_all | solution.py:51
  79.3 19.3 %all-to-all-start.1 = ((bf16[16,2,1440]{2,1,0:T(2,128)(2,1)}), bf16[16,2,1440]{2,1,0:T(2,128)(2,1)S(1)}, u32[]{:S(2)}, u32[]{:S(2)}) async-start(bf16[16,2,1440]{2,1,0:T(2,128)(2,1)} %reshape.165), calls=%async_computation.1 | async-start | bytes 196608 | tf_op jit(solution)/shard_map/all_to_all | solution.py:53
  119.2 16.3 %copy-start.1 = (bf16[2048,192]{0,1:T(8,128)(2,1)S(1)}, bf16[2048,192]{0,1:T(8,128)(2,1)}, u32[]{:S(2)}) copy-start(bf16[2048,192]{0,1:T(8,128)(2,1)} %convert_element_type.255) | copy-start | bytes 2359300
  197.1 13.7 %all-to-all-start.5 = ((bf16[16,2,1440]{2,1,0:T(2,128)(2,1)}), bf16[16,2,1440]{2,1,0:T(2,128)(2,1)S(1)}, u32[]{:S(2)}, u32[]{:S(2)}) async-start(bf16[16,2,1440]{2,1,0:T(2,128)(2,1)} %reshape.173), calls=%async_computation.5 | async-start | bytes 196608 | tf_op jit(solution)/shard_map/all_to_all | solution.py:53
  202.2 276.1 %all-gather.3.cloned.1.call-start = ((), (), s32[]{:S(2)}) async-start(), calls=%async_computation.8 | async-start | bytes 36864000 | tf_op jit(solution)/shard_map/all_gather | solution.py:81
  214.7 5.4 %copy-start.3 = (f32[24,24,3,20]{0,1,2,3:T(8,128)S(1)}, f32[24,24,3,20]{0,1,2,3:T(8,128)}, u32[]{:S(2)}) copy-start(f32[24,24,3,20]{0,1,2,3:T(8,128)} %get-tuple-element.19) | copy-start | bytes 414724
  242.1 87.6 %all-to-all-start.7 = ((bf16[4,2,15360]{2,1,0:T(2,128)(2,1)}), bf16[4,2,15360]{2,1,0:T(2,128)(2,1)S(1)}, u32[]{:S(2)}, u32[]{:S(2)}) async-start(bf16[4,2,15360]{2,1,0:T(2,128)(2,1)} %reshape.177), calls=%async_computation.7 | async-start | bytes 491520 | tf_op jit(solution)/shard_map/all_to_all | solution.py:60
  337.2 7.0 %copy-start.2 = (bf16[1,16,2,20,2048]{4,3,2,1,0:T(8,128)(2,1)S(1)}, bf16[1,16,2,20,2048]{4,3,2,1,0:T(8,128)(2,1)}, u32[]{:S(2)}) copy-start(bf16[1,16,2,20,2048]{4,3,2,1,0:T(8,128)(2,1)} %fusion.4) | copy-start | bytes 7864324
Sparse Core Ops, SparseCore 0:
  220.3 258.0 all-gather.2
